TPU v7x, 32 devices: a whole 2x2x4 slice. The times are simulated.
32 devices in a mesh: rep: 4 (over y, x), row: 2 (over core), col: 4 (over z).
Axes of the slice: x: 2, y: 2, z: 4, core: 2. Of those that a mesh axis runs over, the one named last changes fastest.
Arguments:
- acts: bfloat16 [4, 256, 5120], P('rep', None, 'row'), may hold values from -6 to 6
- grad_out: bfloat16 [4, 256, 13824], P('rep', None, 'col'), may hold values from -0.375 to 0.375
- momentum: bfloat16 [4, 5120, 13824], P('rep', 'row', 'col'), may hold values from -6 to 6
- q_basis: bfloat16 [640, 13824], P(None, 'col'), may hold values from -6 to 6
Outputs:
- momentum_next: bfloat16 [4, 5120, 13824], P('rep', 'row', 'col')
- q_next: bfloat16 [640, 13824], P('row', 'col')
- update: bfloat16 [5120, 13824], P('row', 'col')
All inputs are finite; a program needn't handle non-finite values.
Results may differ from a plain program's by a relative error of at most 0.019.
Values may be sent and summed in bfloat16 or wider, within the bound.
A program may use at most 128 MiB of HBM per device.

v0:
```python
import jax
import jax.numpy as jnp
from jax import lax
from jax.sharding import PartitionSpec as P

RANK = 640


keep_factor = 0.6


def orthonormal(left, gram):
    chol = jnp.linalg.cholesky(gram)
    return lax.linalg.triangular_solve(
        chol, left, left_side=False, lower=True, transpose_a=True
    ).astype(jnp.bfloat16)


def shards(acts, grad_out, momentum, q_basis):
    grad = lax.dot_general(
        acts[0], grad_out[0], (((0,), (0,)), ((), ())), preferred_element_type=jnp.float32
    )
    boosted = (momentum[0].astype(jnp.float32) + grad).astype(jnp.bfloat16)
    partial_value = lax.dot_general(
        boosted, q_basis, (((1,), (1,)), ((), ())), preferred_element_type=jnp.float32
    )
    left = lax.psum(partial_value, ("rep", "col"))
    gram = lax.psum(jnp.dot(left.T, left, precision=lax.Precision.HIGHEST), "row")
    ortho = orthonormal(left, gram)
    replicas = lax.axis_size("rep")
    pooled = lax.psum_scatter(
        boosted.astype(jnp.float32).astype(jnp.bfloat16), "rep", scatter_dimension=1, tiled=True
    ).astype(jnp.float32)
    columns = ortho.astype(jnp.float32)
    summed = lax.psum_scatter(
        lax.dot_general(
            columns,
            pooled,
            (((0,), (0,)), ((), ())),
            precision=lax.Precision.HIGHEST,
            preferred_element_type=jnp.float32,
        ).astype(jnp.bfloat16),
        "row",
        scatter_dimension=0,
        tiled=True,
    ).astype(jnp.float32)
    piece = (summed * (1.0 / replicas)).astype(jnp.bfloat16)
    ranked = lax.all_gather(piece, "row", axis=0, tiled=True)
    right = lax.all_gather(ranked, "rep", axis=1, tiled=True)
    right_wide = right.astype(jnp.float32)
    columns_all = right.shape[1] * lax.axis_size("col")
    squares = lax.psum(jnp.sum(right_wide * right_wide, axis=1), "col")
    msq = squares / columns_all
    q_full = (right_wide * lax.rsqrt(msq + 1e-06)[:, None]).astype(jnp.bfloat16)
    block = RANK // lax.axis_size("row")
    q_next = lax.dynamic_slice_in_dim(q_full, lax.axis_index("row") * block, block, 0)
    feedback = jnp.dot(ortho, right, preferred_element_type=jnp.float32)
    momentum_next = (boosted.astype(jnp.float32) - (1.0 - keep_factor) * feedback).astype(
        jnp.bfloat16
    )[None]
    width_all = boosted.shape[0] * lax.axis_size("row")
    update = (
        jnp.sqrt(jnp.float32(width_all) / RANK)
        * jnp.dot(ortho, q_full, preferred_element_type=jnp.float32)
    ).astype(jnp.bfloat16)
    return (momentum_next, q_next, update)


def solution(mesh):
    in_specs = (
        P("rep", None, "row"),
        P("rep", None, "col"),
        P("rep", "row", "col"),
        P(None, "col"),
    )
    out_specs = (P("rep", "row", "col"), P("row", "col"), P("row", "col"))
    return jax.shard_map(shards, mesh=mesh, in_specs=in_specs, out_specs=out_specs, check_vma=False)
```

profile of v0, /device:TPU:0, one launch (start us, length us, event | category | flops | bytes accessed | tf_op | source)
XLA Modules:
  0.0 697.6 jit_solution(8249359880922253585)
XLA Ops:
  8.1 1.4 copy-done
  9.5 16.3 %fusion = bf16[2560,3456]{1,0:T(8,128)(2,1)} fusion(bf16[1,2560,3456]{2,1,0:T(8,128)(2,1)} %param.6, bf16[1,256,3456]{2,1,0:T(8,128)(2,1)S(1)} %copy-done, bf16[1,256,2560]{2,1,0:T(8,128)(2,1)} %param.4), kind=kOutput, calls=%fused_computation.3 | convolution fusion | flops 4556390400 | bytes 38469632 | tf_op jit(solution)/shard_map/dot_general | solution.py:20
  25.8 19.6 %fusion.64 = f32[2560,640]{1,0:T(8,128)} fusion(bf16[2560,3456]{1,0:T(8,128)(2,1)} %fusion, bf16[640,3456]{1,0:T(8,128)(2,1)} %param.7), kind=kOutput, calls=%fused_computation.112 | convolution fusion | flops 11324620800 | bytes 28672000 | tf_op jit(solution)/shard_map/dot_general | solution.py:24
  45.7 218.5 %all-reduce.4.cloned.1.call-done = f32[2560,640]{1,0:T(8,128)} async-done(((f32[2560,640]{1,0:T(8,128)}), f32[2560,640]{1,0:T(8,128)}) %all-reduce.4.cloned.1.call-update) | async-done | bytes 6553616 | tf_op jit(solution)/shard_map/psum | solution.py:27
  264.2 22.1 %fusion.65 = f32[640,640]{0,1:T(8,128)} fusion(f32[2560,640]{1,0:T(8,128)} %all-reduce.4.cloned.1.call-done), kind=kOutput, calls=%fused_computation.113 | convolution fusion | flops 12582912000 | bytes 8192000 | tf_op jit(solution)/shard_map/dot_general | solution.py:28
  286.3 23.2 %copy.14 = bf16[2560,3456]{0,1:T(8,128)(2,1)} copy(bf16[2560,3456]{1,0:T(8,128)(2,1)} %fusion) | data formatting | bytes 35389440
  309.7 0.5 iota_multiply_fusion
  310.2 2.6 copy.10
  313.0 1.2 copy-done.3
  314.2 11.7 %cholesky.133 = f32[128,128]{1,0:T(8,128)S(1)} custom-call(f32[128,128]{1,0:T(8,128)S(1)} %cholesky.340), custom_call_target="Cholesky" | custom-call | tf_op jit(solution)/shard_map/jit(cholesky)/cholesky | solution.py:13
  325.9 9.8 %custom-call.38 = f32[1,128,128]{1,2,0:T(8,128)S(1)} custom-call(f32[1,128,128]{2,1,0:T(8,128)S(1)} %get-tuple-element.36), custom_call_target="InvertDiagBlocksLowerTriangular" | custom-call | tf_op jit(solution)/shard_map/jit(cholesky)/cholesky | solution.py:13
  336.2 0.4 convolution_subtract_fusion.2
  336.6 0.7 copy-done.5
  337.3 11.7 %cholesky.272 = f32[128,128]{1,0:T(8,128)S(1)} custom-call(f32[128,128]{1,0:T(8,128)S(1)} %cholesky.344), custom_call_target="Cholesky" | custom-call | tf_op jit(solution)/shard_map/jit(cholesky)/cholesky | solution.py:13
  349.1 9.9 %custom-call.39 = f32[1,128,128]{1,2,0:T(8,128)S(1)} custom-call(f32[1,128,128]{2,1,0:T(8,128)S(1)} %get-tuple-element.33), custom_call_target="InvertDiagBlocksLowerTriangular" | custom-call | tf_op jit(solution)/shard_map/jit(cholesky)/cholesky | solution.py:13
  359.0 1.3 convolution_dynamic-update-slice_fusion
  360.3 0.5 convolution_subtract_fusion.3
  360.8 0.7 copy-done.6
  361.5 11.7 %cholesky.293 = f32[128,128]{1,0:T(8,128)S(1)} custom-call(f32[128,128]{1,0:T(8,128)S(1)} %cholesky.349), custom_call_target="Cholesky" | custom-call | tf_op jit(solution)/shard_map/jit(cholesky)/cholesky | solution.py:13
  373.3 9.8 %custom-call.40 = f32[1,128,128]{1,2,0:T(8,128)S(1)} custom-call(f32[1,128,128]{2,1,0:T(8,128)S(1)} %get-tuple-element.30), custom_call_target="InvertDiagBlocksLowerTriangular" | custom-call | tf_op jit(solution)/shard_map/jit(cholesky)/cholesky | solution.py:13
  383.1 1.2 convolution_dynamic-update-slice_fusion.1
  384.3 0.5 convolution_subtract_fusion.4
  384.8 11.7 %cholesky.312 = f32[128,128]{1,0:T(8,128)S(1)} custom-call(f32[128,128]{1,0:T(8,128)S(1)} %cholesky.354), custom_call_target="Cholesky" | custom-call | tf_op jit(solution)/shard_map/jit(cholesky)/cholesky | solution.py:13
  396.7 9.8 %custom-call.41 = f32[1,128,128]{1,2,0:T(8,128)S(1)} custom-call(f32[1,128,128]{2,1,0:T(8,128)S(1)} %get-tuple-element.27), custom_call_target="InvertDiagBlocksLowerTriangular" | custom-call | tf_op jit(solution)/shard_map/jit(cholesky)/cholesky | solution.py:13
  407.1 11.7 %cholesky.329 = f32[128,128]{1,0:T(8,128)S(1)} custom-call(f32[128,128]{1,0:T(8,128)S(1)} %convolution_subtract_fusion.5), custom_call_target="Cholesky" | custom-call | tf_op jit(solution)/shard_map/jit(cholesky)/cholesky | solution.py:13
  418.8 0.7 compare_reduce_fusion.3
  420.8 0.6 compare_reduce_fusion.2
  422.1 0.6 compare_reduce_fusion.1
  423.4 0.6 compare_reduce_fusion
  424.8 0.5 copy-done.7
  425.3 13.1 %while.1 = (s32[]{:T(128)}, f32[640,640]{1,0:T(8,128)S(1)}, s32[5,2]{0,1:T(2,128)S(1)}, f32[5,128,128]{2,1,0:T(8,128)}, s32[]{:T(128)}) while((s32[]{:T(128)}, f32[640,640]{1,0:T(8,128)S(1)}, s32[5,2]{0,1:T(2,128)S(1)}, f32[5,128,128]{2,1,0:T(8,128)}, s32[]{:T(128)}) %tuple.38), condition=%wide.while_cond, body=%wide.while_body.sunk | while | flops 2 | bytes 132205 | solution.py:14
  425.4 0.5 fusion.82
  425.9 2.0 bitcast_dynamic-update-slice_fusion.2
  428.0 0.5 fusion.82
  428.6 2.0 bitcast_dynamic-update-slice_fusion.2
  430.6 0.5 fusion.82
  431.2 2.0 bitcast_dynamic-update-slice_fusion.2
  433.2 0.5 fusion.82
  433.8 2.0 bitcast_dynamic-update-slice_fusion.2
  435.8 0.5 fusion.82
  436.4 2.0 bitcast_dynamic-update-slice_fusion.2
  438.4 50.3 %custom-call.42 = f32[5,128,128]{1,2,0:T(8,128)S(1)} custom-call(f32[5,128,128]{2,1,0:T(8,128)} %get-tuple-element.10), custom_call_target="InvertDiagBlocksLowerTriangular" | custom-call | tf_op jit(solution)/shard_map/triangular_solve | solution.py:14
  488.7 3.5 convert_dynamic-update-slice_fusion.3
  492.2 3.5 convolution_subtract_fusion
  495.7 2.2 convert_dynamic-update-slice_fusion.2
  497.9 5.8 convolution_subtract_fusion.1
  503.7 2.2 convert_dynamic-update-slice_fusion.1
  505.9 8.3 %fusion.20 = f32[2560,128]{1,0:T(8,128)S(1)} fusion(f32[2560,128]{0,1:T(8,128)S(1)} %get-tuple-element.44, f32[2560,128]{0,1:T(8,128)S(1)} %get-tuple-element.42, f32[2560,128]{0,1:T(8,128)S(1)} %get-tuple-element.40, f32[2560,640]{1,0:T(8,128)} %all-reduce.4.cloned.1.call-done, f32[640,640]{1,0:T(8,128)S(1)} %get-tuple-element.108), kind=kOutput, calls=%fused_computation.28 | convolution fusion | flops 1512243200 | bytes 6750208 | tf_op jit(solution)/shard_map/triangular_solve | solution.py:14
  514.2 2.2 convert_dynamic-update-slice_fusion
  516.4 10.3 %fusion.23 = f32[2560,128]{1,0:T(8,128)S(1)} fusion(f32[2560,128]{0,1:T(8,128)S(1)} %get-tuple-element.46, f32[2560,128]{0,1:T(8,128)S(1)} %get-tuple-element.44, f32[2560,128]{0,1:T(8,128)S(1)} %get-tuple-element.42, f32[2560,128]{0,1:T(8,128)S(1)} %get-tuple-element.40, f32[2560,640]{1,0:T(8,128)} %all-reduce.4.cloned.1.call-done, ...), kind=kOutput, calls=%fused_computation.30 | convolution fusion | flops 2017525760 | bytes 8126464 | tf_op jit(solution)/shard_map/triangular_solve | solution.py:14
  526.7 2.2 fusion.26
  528.9 7.8 %fusion.32 = bf16[640,864]{1,0:T(8,128)(2,1)} fusion(bf16[2560,640]{0,1:T(8,128)(2,1)} %fusion.26, bf16[864,2560]{1,0:T(8,128)(2,1)} %reduce-scatter.7.cloned.1.call-done), kind=kOutput, calls=%fused_computation.41 | convolution fusion | flops 2831708160 | bytes 8806400 | tf_op jit(solution)/shard_map/dot_general | solution.py:36
  536.8 9.4 %reduce-scatter.5.cloned.1.call-done = bf16[320,864]{1,0:T(8,128)(2,1)} async-done(((bf16[640,864]{1,0:T(8,128)(2,1)}), bf16[320,864]{1,0:T(8,128)(2,1)}) %reduce-scatter.5.cloned.1.call-update) | async-done | bytes 552976 | tf_op jit(solution)/shard_map/reduce_scatter | solution.py:35
  546.2 2.0 multiply_convert_fusion.1
  548.2 10.5 %all-gather.3.cloned.1.call-done = bf16[640,864]{1,0:T(8,128)(2,1)} async-done(((bf16[320,864]{1,0:T(8,128)(2,1)}), bf16[640,864]{1,0:T(8,128)(2,1)}) %all-gather.3.cloned.1.call-update) | async-done | bytes 1105936 | tf_op jit(solution)/shard_map/all_gather | solution.py:48
  558.7 2.4 copy.11
  561.1 55.7 %all-gather.5.cloned.1.call-done = bf16[640,3456]{0,1:T(8,128)(2,1)} async-done(((bf16[640,864]{0,1:T(8,128)(2,1)}), bf16[640,3456]{0,1:T(8,128)(2,1)}) %all-gather.5.cloned.1.call-update) | async-done | bytes 4423696 | tf_op jit(solution)/shard_map/all_gather | solution.py:49
  616.8 3.2 fusion.2
  620.0 11.7 %psum.23 = f32[640]{0:T(1024)S(1)} all-reduce(f32[640]{0:T(1024)S(1)} %fusion.2), channel_id=1, replica_groups=mesh['rep'=4,'row'=2,'col'=4] {'col'}, use_global_device_ids=true, to_apply=%region_15.16 | all-reduce | flops 640 | bytes 5120 | tf_op jit(solution)/shard_map/psum | solution.py:52
  631.7 5.2 fusion.3
  636.9 21.1 %multiply_convert_fusion = bf16[2560,3456]{1,0:T(8,128)(2,1)} fusion(bf16[2560,640]{0,1:T(8,128)(2,1)} %fusion.26, bf16[640,3456]{0,1:T(8,128)(2,1)} %fusion.3), kind=kOutput, calls=%fused_computation.4 | convolution fusion | flops 11342315520 | bytes 25395200 | tf_op jit(solution)/shard_map/dot_general | solution.py:64
  658.0 5.0 constant_dynamic-slice_fusion.1
  663.0 4.3 copy.12
  667.3 22.7 %fusion.1 = bf16[1,2560,3456]{2,1,0:T(8,128)(2,1)} fusion(bf16[2560,640]{0,1:T(8,128)(2,1)} %fusion.26, bf16[640,3456]{0,1:T(8,128)(2,1)} %all-gather.5.cloned.1.call-done, bf16[2560,3456]{1,0:T(8,128)(2,1)} %fusion), kind=kOutput, calls=%fused_computation.6 | convolution fusion | flops 11360010240 | bytes 43089920 | tf_op jit(solution)/shard_map/dot_general | solution.py:57
  (48 shorter events, 2.5 us)
Async XLA Ops:
  8.0 1.5 copy-start
  8.0 256.2 %all-reduce.4.cloned.1.call-start = ((), (), s32[]{:S(2)}) async-start(), calls=%async_computation.2 | async-start | bytes 13107200 | tf_op jit(solution)/shard_map/psum | solution.py:27
  45.4 264.8 %all-reduce.6.cloned.1.call-start = ((), (), s32[]{:S(2)}) async-start(), calls=%async_computation.3 | async-start | bytes 3276800 | tf_op jit(solution)/shard_map/psum | solution.py:28
  286.3 242.6 %reduce-scatter.7.cloned.1.call-start = ((), (), s32[]{:S(2)}) async-start(), calls=%async_computation.7 | async-start | bytes 22118400
  309.6 236.6 %reduce-scatter.5.cloned.1.call-start = ((), (), s32[]{:S(2)}) async-start(), calls=%async_computation.4 | async-start | bytes 1720320 | tf_op jit(solution)/shard_map/reduce_scatter | solution.py:35
  310.2 2.6 copy-start.2
  313.0 1.2 copy-start.3
  314.2 21.7 %copy-start.4 = (f32[640,640]{1,0:T(8,128)S(1)}, f32[640,640]{1,0:T(8,128)}, u32[]{:S(2)}) copy-start(f32[640,640]{1,0:T(8,128)} %copy-done.3) | copy-start | bytes 4915204
  336.6 0.7 copy-start.5
  360.8 0.7 copy-start.6
  424.7 0.6 copy-start.7
  536.7 21.9 %all-gather.3.cloned.1.call-start = ((), (), s32[]{:S(2)}) async-start(), calls=%async_computation.5 | async-start | bytes 1720320 | tf_op jit(solution)/shard_map/all_gather | solution.py:48
  548.2 68.6 %all-gather.5.cloned.1.call-start = ((), (), s32[]{:S(2)}) async-start(), calls=%async_computation.6 | async-start | bytes 5529600 | tf_op jit(solution)/shard_map/all_gather | solution.py:49
  667.3 22.7 %copy-start.1 = (bf16[1,256,3456]{2,1,0:T(8,128)(2,1)S(1)}, bf16[1,256,3456]{2,1,0:T(8,128)(2,1)}, u32[]{:S(2)}) copy-start(bf16[1,256,3456]{2,1,0:T(8,128)(2,1)} %param.5) | copy-start | bytes 5308420
Sparse Core Ops, SparseCore 0:
  45.5 218.5 all-reduce.3
  286.4 19.5 all-reduce.5
  536.9 9.2 reduce-scatter.4
  548.3 10.3 all-gather.2
Sparse Core Ops, SparseCore 1:
  309.7 161.9 reduce-scatter.6
  561.1 55.6 all-gather.4
where the time goes:
time: 703 us; the launch traced here: 698 us
  waiting for transfers between devices  294 us (42%)
  other arithmetic  162 us (23%)
  matrix products  154 us (22%)
  local copies, waits for them, and re-layouts  55.1 us (8%)
  between operations  19.4 us (3%)
  blocking collectives  11.7 us (2%)
    psum x1, waiting for transfers between devices, shards(): left = lax.psum(partial_value, ('rep', 'col'))  218 us
    another operation x18, other arithmetic, orthonormal(): chol = jnp.linalg.cholesky(gram)  101 us
    all_gather x1, waiting for transfers between devices, shards(): right = lax.all_gather(ranked, 'rep', axis=1, tiled=True)  55.7 us
    another operation x3, other arithmetic, orthonormal(): lax.linalg.triangular_solve(chol, left, left_side=False, lower=True, tran...  51 us
    another operation x9, matrix products, orthonormal(): lax.linalg.triangular_solve(chol, left, left_side=False, lower=True, tran...  40.1 us
    unnamed x18, local copies, waits for them, and re-layouts  32 us
    dot_general x1, matrix products, shards(): feedback = jnp.dot(ortho, right, preferred_element_type=jnp.float32)  22.7 us
    dot_general x1, matrix products, shards(): jnp.dot(left.T, left, precision=lax.Precision.HIGHEST)  22.1 us
  transfers between devices with their start and end apart: 6, of which 4 were waited for; matrix products, arithmetic and copies ran while one was open for 34% of the time, Pallas kernels for 0%

commit v1 on v0

v1 whole, which is shorter than its diff:
```python
import functools

import jax
import jax.numpy as jnp
from jax import lax
from jax.experimental import pallas as pl
from jax.experimental.pallas import tpu as pltpu
from jax.sharding import PartitionSpec as P

BLOCK = 128
TILE = 8

keep_factor = 0.6


def dot_f32(a, b, dims):
    return lax.dot_general(
        a, b, (dims, ((), ())), precision=lax.Precision.HIGHEST, preferred_element_type=jnp.float32
    )


def block_factor(block):
    lane = lax.broadcasted_iota(jnp.int32, (1, BLOCK), 1)
    sub = lax.broadcasted_iota(jnp.int32, (TILE, 1), 0)
    tiles = [block[t * TILE : (t + 1) * TILE] for t in range(BLOCK // TILE)]
    for k in range(BLOCK):
        at, r = divmod(k, TILE)
        here = lane == k
        row = tiles[at][r : r + 1]
        scale = lax.rsqrt(jnp.broadcast_to(row[:, k : k + 1], (1, BLOCK)))
        done = jnp.where(here, 1.0, row) * scale
        used = done * scale
        tile = tiles[at]
        later = jnp.where(here, 0.0, tile) - tile[:, k : k + 1] * used
        tiles[at] = jnp.where(sub == r, done, jnp.where(sub > r, later, tile))
        for t in range(at + 1, len(tiles)):
            tile = tiles[t]
            tiles[t] = jnp.where(here, 0.0, tile) - tile[:, k : k + 1] * used
    whole = jnp.concatenate(tiles, axis=0)
    rows = lax.broadcasted_iota(jnp.int32, (BLOCK, BLOCK), 0)
    cols = lax.broadcasted_iota(jnp.int32, (BLOCK, BLOCK), 1)
    return jnp.where(rows >= cols, whole, 0.0)


def inverse_kernel(gram_ref, high_ref, low_ref, work):
    size = gram_ref.shape[0]
    work[...] = gram_ref[...]
    row_at = lax.broadcasted_iota(jnp.int32, (size, 1), 0)

    def step(j, carry):
        at = pl.ds(pl.multiple_of(j * BLOCK, BLOCK), BLOCK)
        factor = block_factor(work[at, at])
        panel = dot_f32(work[:, at], factor, ((1,), (1,)))
        panel = jnp.where(row_at >= (j + 1) * BLOCK, panel, 0.0)
        work[at, :] = dot_f32(factor, work[at, :], ((1,), (0,)))
        work[at, at] = factor
        rest = row_at >= (j + 1) * BLOCK
        work[:, at] = jnp.where(rest, 0.0, work[:, at])
        work[...] -= dot_f32(panel, work[at, :], ((1,), (0,)))
        return carry

    lax.fori_loop(0, size // BLOCK, step, 0)
    rows = lax.broadcasted_iota(jnp.int32, (size, size), 0)
    cols = lax.broadcasted_iota(jnp.int32, (size, size), 1)
    inverse = jnp.where(rows >= cols, work[...], 0.0)
    high = inverse.astype(jnp.bfloat16)
    high_ref[...] = high
    low_ref[...] = (inverse - high.astype(jnp.float32)).astype(jnp.bfloat16)


def inverse_factor(gram):
    size = gram.shape[0]
    return pl.pallas_call(
        inverse_kernel,
        out_shape=[jax.ShapeDtypeStruct((size, size), jnp.bfloat16)] * 2,
        in_specs=[pl.BlockSpec(memory_space=pltpu.VMEM)],
        out_specs=[pl.BlockSpec(memory_space=pltpu.VMEM)] * 2,
        scratch_shapes=[pltpu.VMEM((size, size), jnp.float32)],
        compiler_params=pltpu.CompilerParams(vmem_limit_bytes=24 * 1024 * 1024),
        cost_estimate=pl.CostEstimate(
            flops=60_000_000_000, bytes_accessed=6 * size * size, transcendentals=size
        ),
        name="inverse_factor",
    )(gram)


def matmul(a, b, dims):
    return lax.dot_general(a, b, (dims, ((), ())), preferred_element_type=jnp.float32)


def shards(acts, grad_out, momentum, q_basis):
    grad = matmul(acts[0], grad_out[0], ((0,), (0,)))
    boosted = (momentum[0].astype(jnp.float32) + grad).astype(jnp.bfloat16)
    partial_value = matmul(boosted, q_basis, ((1,), (1,))).astype(jnp.bfloat16)
    piece = lax.psum_scatter(partial_value, "rep", scatter_dimension=0, tiled=True)
    piece = lax.psum_scatter(piece, "col", scatter_dimension=0, tiled=True)
    piece = lax.all_gather(piece, "col", axis=0, tiled=True)
    left = lax.all_gather(piece, "rep", axis=0, tiled=True)
    gram_part, left = lax.optimization_barrier((matmul(left, left, ((0,), (0,))), left))
    gram = lax.psum(gram_part, "row")
    replicas = lax.axis_size("rep")
    moved = matmul(left, boosted, ((0,), (0,))).astype(jnp.bfloat16)
    gram, moved = lax.optimization_barrier((gram, moved))
    moved = lax.psum(moved, ("row", "rep"))
    high, low = inverse_factor(gram)
    right_sum = matmul(high, moved, ((1,), (0,))) + matmul(low, moved, ((1,), (0,)))
    right = (right_sum * (1.0 / replicas)).astype(jnp.bfloat16)
    ortho = (matmul(left, high, ((1,), (1,))) + matmul(left, low, ((1,), (1,)))).astype(
        jnp.bfloat16
    )
    right_wide = right.astype(jnp.float32)
    columns_all = right.shape[1] * lax.axis_size("col")
    squares = lax.psum(jnp.sum(right_wide * right_wide, axis=1), "col")
    feedback = matmul(ortho, right, ((1,), (0,)))
    momentum_next = (boosted.astype(jnp.float32) - (1.0 - keep_factor) * feedback).astype(
        jnp.bfloat16
    )[None]
    msq = squares / columns_all
    q_full = (right_wide * lax.rsqrt(msq + 1e-06)[:, None]).astype(jnp.bfloat16)
    rank = q_basis.shape[0]
    block = rank // lax.axis_size("row")
    q_next = lax.dynamic_slice_in_dim(q_full, lax.axis_index("row") * block, block, 0)
    width_all = boosted.shape[0] * lax.axis_size("row")
    update = (
        jnp.sqrt(jnp.float32(width_all) / rank) * matmul(ortho, q_full, ((1,), (0,)))
    ).astype(jnp.bfloat16)
    return (momentum_next, q_next, update)


def solution(mesh):
    in_specs = (
        P("rep", None, "row"),
        P("rep", None, "col"),
        P("rep", "row", "col"),
        P(None, "col"),
    )
    out_specs = (P("rep", "row", "col"), P("row", "col"), P("row", "col"))
    return jax.shard_map(shards, mesh=mesh, in_specs=in_specs, out_specs=out_specs, check_vma=False)
```

time: 703 us -> 382 us (0.54)
  waiting for transfers between devices: 294 us -> 135 us
  other arithmetic: 162 us -> 3.64 us
  Pallas kernels: 0 us -> 66.9 us
  local copies, waits for them, and re-layouts: 55.1 us -> 4.38 us
  matrix products: 154 us -> 121 us
  blocking collectives: 11.7 us -> 30.5 us
    psum x2, waiting for transfers between devices: 219 us -> 16.5 us  [the longest x1 14.3 us: shards(): moved = lax.psum(moved, ('row', 'rep'))]
    another operation x21 -> x0, other arithmetic: 152 us -> none  [the longest x18 101 us: orthonormal(): chol = jnp.linalg.cholesky(gram)]
    pallas_call x0 -> x1, Pallas kernels: none -> 66.9 us  [inverse_factor(): pl.pallas_call(inverse_kernel, out_shape=[jax.ShapeDtypeStruct((size, siz...]
    reduce_scatter x1 -> x2, waiting for transfers between devices: 9.37 us -> 73.8 us  [the longest x1 47.9 us: shards(): lax.psum_scatter(partial_value, 'rep', scatter_dimension=0, tiled=True)]
    another operation x17 -> x0, matrix products: 44.9 us -> none  [the longest x9 40.1 us: orthonormal(): lax.linalg.triangular_solve(chol, left, left_side=False, lower=True, tran...]
    unnamed x18 -> x12, local copies, waits for them, and re-layouts: 32 us -> 2.87 us
    all_gather x2 -> x1, waiting for transfers between devices: 66.2 us -> 44.5 us  [shards(): left = lax.all_gather(piece, 'rep', axis=0, tiled=True)]
    all_gather x0 -> x1, blocking collectives: none -> 18.9 us  [shards(): piece = lax.all_gather(piece, 'col', axis=0, tiled=True)]
  transfers between devices with their start and end apart: 6 -> 5, of which waited for: 4 -> 5; matrix products, arithmetic and copies ran while one was open for 34% -> 7% of each run, Pallas kernels for 0% -> 18%
where the time goes in v1:
time: 382 us; the launch traced here: 376 us
  waiting for transfers between devices  135 us (35%)
  matrix products  121 us (32%)
  Pallas kernels  66.9 us (18%)
  blocking collectives  30.5 us (8%)
  between operations  14.3 us (4%)
  local copies, waits for them, and re-layouts  4.38 us (1%)
    dot_general x10, matrix products, matmul(): lax.dot_general(a, b, (dims, ((), ())), preferred_element_type=jnp.float32)  121 us
    pallas_call x1, Pallas kernels, inverse_factor(): pl.pallas_call(inverse_kernel, out_shape=[jax.ShapeDtypeStruct((size, siz...  66.9 us
    reduce_scatter x1, waiting for transfers between devices, shards(): lax.psum_scatter(partial_value, 'rep', scatter_dimension=0, tiled=True)  47.9 us
    all_gather x1, waiting for transfers between devices, shards(): left = lax.all_gather(piece, 'rep', axis=0, tiled=True)  44.5 us
    reduce_scatter x1, waiting for transfers between devices, shards(): piece = lax.psum_scatter(piece, 'col', scatter_dimension=0, tiled=True)  25.9 us
    all_gather x1, blocking collectives, shards(): piece = lax.all_gather(piece, 'col', axis=0, tiled=True)  18.9 us
    psum x1, waiting for transfers between devices, shards(): moved = lax.psum(moved, ('row', 'rep'))  14.3 us
    psum x1, blocking collectives, shards(): squares = lax.psum(jnp.sum(right_wide * right_wide, axis=1), 'col')  11.7 us
  transfers between devices with their start and end apart: 5, of which 5 were waited for; matrix products, arithmetic and copies ran while one was open for 7% of the time, Pallas kernels for 18%

profile of v1, /device:TPU:0, one launch (start us, length us, event | category | flops | bytes accessed | tf_op | source)
XLA Modules:
  0.0 376.2 jit_solution(15955420044553961625)
XLA Ops:
  7.2 0.0 copy-start
  7.2 0.0 reduce-scatter.3.cloned.1.call-start
  7.2 1.4 copy-done
  8.6 16.4 %fusion = bf16[2560,3456]{1,0:T(8,128)(2,1)} fusion(bf16[1,2560,3456]{2,1,0:T(8,128)(2,1)} %param.6, bf16[1,256,3456]{2,1,0:T(8,128)(2,1)S(1)} %copy-done, bf16[1,256,2560]{2,1,0:T(8,128)(2,1)} %param.4), kind=kOutput, calls=%fused_computation.1 | convolution fusion | flops 4556390400 | bytes 38469632 | tf_op jit(solution)/shard_map/dot_general | solution.py:88
  25.0 19.9 %convolution_convert_fusion.1 = bf16[2560,640]{1,0:T(8,128)(2,1)} fusion(bf16[2560,3456]{1,0:T(8,128)(2,1)} %fusion, bf16[640,3456]{1,0:T(8,128)(2,1)} %param.7), kind=kOutput, calls=%fused_computation.12 | convolution fusion | flops 11326259200 | bytes 25395200 | tf_op jit(solution)/shard_map/dot_general | solution.py:88
  44.9 0.0 reduce-scatter.3.cloned.1.call-update
  44.9 0.0 reduce-scatter.5.cloned.1.call-start
  45.0 47.9 %reduce-scatter.3.cloned.1.call-done = bf16[640,640]{1,0:T(8,128)(2,1)} async-done(((bf16[2560,640]{1,0:T(8,128)(2,1)}), bf16[640,640]{1,0:T(8,128)(2,1)}) %reduce-scatter.3.cloned.1.call-update) | async-done | bytes 819216 | tf_op jit(solution)/shard_map/reduce_scatter | solution.py:95
  92.9 0.0 reduce-scatter.5.cloned.1.call-update
  92.9 0.0 all-gather.2.cloned.1.call-start
  93.0 25.9 %reduce-scatter.5.cloned.1.call-done = bf16[160,640]{1,0:T(8,128)(2,1)} async-done(((bf16[640,640]{1,0:T(8,128)(2,1)}), bf16[160,640]{1,0:T(8,128)(2,1)}) %reduce-scatter.5.cloned.1.call-update) | async-done | bytes 204816 | tf_op jit(solution)/shard_map/reduce_scatter | solution.py:96
  118.9 18.9 %all_gather.6 = bf16[640,640]{1,0:T(8,128)(2,1)} all-gather(bf16[160,640]{1,0:T(8,128)(2,1)} %reduce-scatter.5.cloned.1.call-done), channel_id=1, replica_groups=mesh['rep'=4,'row'=2,'col'=4] {'col'}, dimensions={0}, use_global_device_ids=true | all-gather | bytes 1024000 | tf_op jit(solution)/shard_map/all_gather | solution.py:97
  137.7 0.0 all-gather.2.cloned.1.call-update
  137.8 0.0 all-reduce.3.cloned.1.call-start
  137.8 44.5 %all-gather.2.cloned.1.call-done = bf16[2560,640]{1,0:T(8,128)(2,1)} async-done(((bf16[640,640]{1,0:T(8,128)(2,1)}), bf16[2560,640]{1,0:T(8,128)(2,1)}) %all-gather.2.cloned.1.call-update) | async-done | bytes 3276816 | tf_op jit(solution)/shard_map/all_gather | solution.py:98
  182.4 6.8 %fusion.6 = f32[640,640]{1,0:T(8,128)} fusion(bf16[2560,640]{1,0:T(8,128)(2,1)} %all-gather.2.cloned.1.call-done), kind=kOutput, calls=%fused_computation.17 | convolution fusion | flops 2097152000 | bytes 4915200 | tf_op jit(solution)/shard_map/dot_general | solution.py:88
  189.2 0.0 all-reduce.3.cloned.1.call-update
  189.2 0.2 all-reduce.5.cloned.1.call-start
  189.5 18.3 %convolution_convert_fusion = bf16[640,3456]{1,0:T(8,128)(2,1)} fusion(bf16[2560,640]{1,0:T(8,128)(2,1)} %all-gather.2.cloned.1.call-done, bf16[2560,3456]{1,0:T(8,128)(2,1)} %fusion), kind=kOutput, calls=%fused_computation.11 | convolution fusion | flops 11326832640 | bytes 25395200 | tf_op jit(solution)/shard_map/dot_general | solution.py:88
  207.8 2.1 all-reduce.3.cloned.1.call-done.gram_ref
  209.9 0.0 all-reduce.5.cloned.1.call-update
  209.9 0.0 copy-start.2
  209.9 1.4 copy-done.2
  211.3 0.0 copy-start.4
  211.4 66.9 %inverse_factor.1 = (bf16[640,640]{1,0:T(8,128)(2,1)S(1)}, bf16[640,640]{1,0:T(8,128)(2,1)S(1)}) custom-call(f32[640,640]{1,0:T(8,128)S(1)} %copy-done.2), custom_call_target="tpu_custom_call" | custom-call | flops 60000002048 | bytes 2457600 | tf_op jit(solution)/shard_map/inverse_factor/pallas_call | solution.py:73
  278.3 0.0 copy-done.4
  278.3 3.1 fusion.7
  281.4 4.5 %add_convert_fusion = bf16[2560,640]{1,0:T(8,128)(2,1)} fusion(f32[2560,640]{1,0:T(8,128)S(1)} %fusion.7, bf16[2560,640]{1,0:T(8,128)(2,1)S(1)} %copy-done.4, bf16[640,640]{1,0:T(8,128)(2,1)S(1)} %get-tuple-element.13), kind=kOutput, calls=%fused_computation.10 | convolution fusion | flops 2100428800 | bytes 13926400 | tf_op jit(solution)/shard_map/dot_general | solution.py:88
  286.0 14.3 %all-reduce.5.cloned.1.call-done = bf16[640,3456]{1,0:T(8,128)(2,1)} async-done(((bf16[640,3456]{1,0:T(8,128)(2,1)}), bf16[640,3456]{1,0:T(8,128)(2,1)}) %all-reduce.5.cloned.1.call-update) | async-done | bytes 4423696 | tf_op jit(solution)/shard_map/psum | solution.py:104
  300.3 0.0 copy-start.3
  300.3 5.8 %fusion.8 = f32[640,3456]{1,0:T(8,128)S(1)} fusion(bf16[640,640]{1,0:T(8,128)(2,1)S(1)} %get-tuple-element.12, bf16[640,3456]{1,0:T(8,128)(2,1)} %all-reduce.5.cloned.1.call-done), kind=kOutput, calls=%fused_computation.19 | convolution fusion | flops 2831155200 | bytes 14090240 | tf_op jit(solution)/shard_map/dot_general | solution.py:88
  306.1 0.0 copy-done.3
  306.1 5.7 %fusion.2 = (f32[640]{0:T(1024)S(1)}, bf16[640,3456]{1,0:T(8,128)(2,1)}) fusion(f32[640,3456]{1,0:T(8,128)S(1)} %fusion.8, bf16[640,640]{1,0:T(8,128)(2,1)S(1)} %get-tuple-element.13, bf16[640,3456]{1,0:T(8,128)(2,1)S(1)} %copy-done.3), kind=kOutput, calls=%fused_computation.7 | convolution fusion | flops 2844425728 | bytes 18516480 | tf_op jit(solution)/shard_map/dot_general | solution.py:88
  311.8 11.7 %psum.23 = f32[640]{0:T(1024)S(1)} all-reduce(f32[640]{0:T(1024)S(1)} %get-tuple-element.15), channel_id=1, replica_groups=mesh['rep'=4,'row'=2,'col'=4] {'col'}, use_global_device_ids=true, to_apply=%region_5.0 | all-reduce | flops 640 | bytes 5120 | tf_op jit(solution)/shard_map/psum | solution.py:113
  323.4 23.7 %fusion.1 = bf16[1,2560,3456]{2,1,0:T(8,128)(2,1)} fusion(bf16[2560,640]{1,0:T(8,128)(2,1)} %add_convert_fusion, bf16[640,3456]{1,0:T(8,128)(2,1)} %get-tuple-element.16, bf16[2560,3456]{1,0:T(8,128)(2,1)} %fusion), kind=kOutput, calls=%fused_computation.4 | convolution fusion | flops 11360010240 | bytes 43089920 | tf_op jit(solution)/shard_map/dot_general | solution.py:88
  347.2 0.0 copy-start.5
  347.2 3.6 fusion.3
  350.8 0.0 copy-done.5
  350.8 0.0 copy-start.1
  350.8 16.9 %multiply_convert_fusion = bf16[2560,3456]{1,0:T(8,128)(2,1)} fusion(bf16[2560,640]{1,0:T(8,128)(2,1)S(1)} %copy-done.5, bf16[640,3456]{1,0:T(8,128)(2,1)S(1)} %fusion.3), kind=kOutput, calls=%fused_computation.2 | convolution fusion | flops 11342315520 | bytes 25395200 | tf_op jit(solution)/shard_map/dot_general | solution.py:88
  367.7 1.5 constant_dynamic-slice_fusion
  369.2 0.0 copy-done.1
  (1 shorter events, 0.0 us)
Async XLA Ops:
  7.2 1.5 copy-start
  7.2 85.7 %reduce-scatter.3.cloned.1.call-start = ((), (), s32[]{:S(2)}) async-start(), calls=%async_computation.2 | async-start | bytes 4096000 | tf_op jit(solution)/shard_map/reduce_scatter | solution.py:95
  44.9 73.9 %reduce-scatter.5.cloned.1.call-start = ((), (), s32[]{:S(2)}) async-start(), calls=%async_computation.3 | async-start | bytes 1024000 | tf_op jit(solution)/shard_map/reduce_scatter | solution.py:96
  92.9 89.5 %all-gather.2.cloned.1.call-start = ((), (), s32[]{:S(2)}) async-start(), calls=%async_computation.4 | async-start | bytes 4096000 | tf_op jit(solution)/shard_map/all_gather | solution.py:98
  137.8 72.1 %all-reduce.3.cloned.1.call-start = ((), (), s32[]{:S(2)}) async-start(), calls=%async_computation.5 | async-start | bytes 3276800 | tf_op jit(solution)/shard_map/psum | solution.py:100
  189.2 111.0 %all-reduce.5.cloned.1.call-start = ((), (), s32[]{:S(2)}) async-start(), calls=%async_computation.6 | async-start | bytes 8847360 | tf_op jit(solution)/shard_map/psum | solution.py:104
  209.9 1.4 copy-start.2
  211.3 66.9 %copy-start.4 = (bf16[2560,640]{1,0:T(8,128)(2,1)S(1)}, bf16[2560,640]{1,0:T(8,128)(2,1)}, u32[]{:S(2)}) copy-start(bf16[2560,640]{1,0:T(8,128)(2,1)} %all-gather.2.cloned.1.call-done) | copy-start | bytes 9830404
  300.3 5.8 %copy-start.3 = (bf16[640,3456]{1,0:T(8,128)(2,1)S(1)}, bf16[640,3456]{1,0:T(8,128)(2,1)}, u32[]{:S(2)}) copy-start(bf16[640,3456]{1,0:T(8,128)(2,1)} %all-reduce.5.cloned.1.call-done) | copy-start | bytes 13271044
  347.2 3.6 copy-start.5
  350.8 18.4 %copy-start.1 = (bf16[1,256,3456]{2,1,0:T(8,128)(2,1)S(1)}, bf16[1,256,3456]{2,1,0:T(8,128)(2,1)}, u32[]{:S(2)}) copy-start(bf16[1,256,3456]{2,1,0:T(8,128)(2,1)} %param.5) | copy-start | bytes 5308420
Sparse Core Ops, SparseCore 0:
  45.0 47.7 reduce-scatter.2
  95.2 23.6 reduce-scatter.4
  137.9 44.4 all-gather.1
  189.4 20.4 all-reduce.2
  214.0 86.1 all-reduce.4
